TPU v7x, 32 devices: a whole 2x2x4 slice. The times are simulated.
32 devices in a mesh: req: 2 (over y), patch: 16 (over z, x, core).
Axes of the slice: x: 2, y: 2, z: 4, core: 2. Of those that a mesh axis runs over, the one named last changes fastest.
Arguments:
- queries: bfloat16 [768, 2560], P(('req', 'patch')), parts along dimension 0, may hold values from -200 to 200, as said below
- stale_kv: bfloat16 [2, 768, 2560], P(None, ('req', 'patch')), parts along dimension 1, may hold values from -6 to 6, as said below
- residual_codes: int32 [2, 768, 2560], P(None, ('req', 'patch')), parts along dimension 1, may hold values from 0 to 255
- scale_exponents: int32 [2, 768, 80], P(None, ('req', 'patch')), parts along dimension 1, may hold values from 6 to 9
Outputs:
- attended: bfloat16 [768, 2560], P(('req', 'patch')), parts along dimension 0
There are 2 independent parts, one for each index of `req`. A program takes and returns all parts, laid end to end along the dimension named above; each array names one. Nothing has to cross between parts.
Inputs may be any that keep to these rules, and one draw needn't show every extreme that they name: `queries`: queries are of order three; a few rows may be far larger. `stale_kv`: keys and values of last step, of order one.
All inputs are finite; a program needn't handle non-finite values.
Results may differ from a plain program's by a relative error of at most 0.0073.
Values may be sent and summed in bfloat16 or wider, within the bound.
A program may use at most 128 MiB of HBM per device.

v0:
```python
import jax
import jax.numpy as jnp
from jax import lax
from jax.sharding import PartitionSpec as P

HEADS = 20
HD = 128
BLOCK = 32


def decode_residual(residual_codes, scale_exponents, width):
    sign_part = 1.0 - 2.0 * (residual_codes // 128).astype(jnp.float32)
    exponent = residual_codes // 8 % 16
    mantissa = (residual_codes % 8).astype(jnp.float32)
    power = jnp.exp2((exponent - 7).astype(jnp.float32))
    normal_value = (1.0 + mantissa / 8.0) * power
    small_value = mantissa / 8.0 * 2.0 ** (-6)
    magnitude = jnp.where(exponent == 0, small_value, normal_value)
    block_scale = jnp.exp2((scale_exponents - 16).astype(jnp.float32))
    shaped = (sign_part * magnitude).reshape(scale_exponents.shape + (width,))
    return (shaped * block_scale[..., None]).reshape(residual_codes.shape)


def per_device(queries, stale_kv, residual_codes, scale_exponents):
    residual = decode_residual(residual_codes, scale_exponents, BLOCK)
    rebuilt = (stale_kv.astype(jnp.float32) + residual).astype(jnp.bfloat16)
    local_rows = queries.shape[0]
    head_query = queries.reshape(local_rows, HEADS, HD)
    score_scale = HD ** (-0.5)
    all_keys, all_values = (
        lax.all_gather(rebuilt[0], "patch", axis=0, tiled=True),
        lax.all_gather(rebuilt[1], "patch", axis=0, tiled=True),
    )
    pieces = (all_keys, all_values)
    row_max = jnp.full((HEADS, local_rows), -1e30, jnp.float32)
    key_piece = pieces[0].reshape(pieces[0].shape[0], HEADS, HD)
    value_piece = pieces[1].reshape(pieces[1].shape[0], HEADS, HD)
    scores = (
        jnp.einsum("qhd,khd->hqk", head_query, key_piece, preferred_element_type=jnp.float32)
        * score_scale
    )
    new_max = jnp.maximum(row_max, jnp.max(scores, axis=2))
    weights_exp = jnp.exp(scores - new_max[..., None])
    new_sum = jnp.sum(weights_exp, axis=2)
    product = jnp.einsum(
        "hqk,khd->hqd",
        weights_exp.astype(jnp.bfloat16),
        value_piece,
        preferred_element_type=jnp.float32,
    )
    final_state = (new_max, new_sum, product)
    row_max, row_sum, weighted = final_state
    result = weighted / row_sum[..., None]
    return result.transpose(1, 0, 2).reshape(local_rows, HEADS * HD).astype(jnp.bfloat16)


def solution(mesh):
    return jax.shard_map(
        per_device,
        mesh=mesh,
        in_specs=(
            P(("req", "patch"), None),
            P(None, ("req", "patch"), None),
            P(None, ("req", "patch"), None),
            P(None, ("req", "patch"), None),
        ),
        out_specs=P(("req", "patch"), None),
        check_vma=False,
    )
```

profile of v0, /device:TPU:0, one launch (start us, length us, event | category | flops | bytes accessed | tf_op | source)
XLA Modules:
  0.0 107.5 jit_solution(15675465119041559300)
XLA Ops:
  6.5 0.0 copy-start
  6.5 0.0 all-gather.5.cloned.1.call-start
  6.5 0.8 multiply_exponential_fusion
  7.3 0.0 copy-start.1
  7.3 0.0 copy-start.2
  7.4 0.6 mul.44
  7.9 0.8 mul.45
  8.7 0.0 copy-done.1
  8.7 0.0 copy-done.2
  8.7 1.1 %fusion.13 = bf16[2,24,2560]{2,1,0:T(8,128)(2,1)S(1)} fusion(f32[2,24,2560]{2,1,0:T(8,128)S(1)} %mul.45, bf16[2,24,2560]{2,1,0:T(8,128)(2,1)S(1)} %copy-done.2, s32[2,24,2560]{2,1,0:T(8,128)S(1)} %copy-done.1), kind=kLoop, calls=%fused_computation.27 | loop fusion | flops 7127040 | bytes 1474560 | tf_op jit(solution)/shard_map/convert_element_type | solution.py:26
  9.8 0.7 fusion.22
  10.5 0.0 all-gather.5.cloned.1.call-update
  10.6 0.0 all-gather.7.cloned.1.call-start
  10.6 0.7 all-gather.7.cloned.1.call-update
  11.3 42.9 %all-gather.5.cloned.1.call-done = bf16[1,384,2560]{2,1,0:T(8,128)(2,1)} async-done(((bf16[1,24,2560]{2,1,0:T(8,128)(2,1)}), bf16[1,384,2560]{2,1,0:T(8,128)(2,1)}) %all-gather.5.cloned.1.call-update) | async-done | bytes 1966096 | tf_op jit(solution)/shard_map/all_gather | solution.py:31
  54.3 2.8 %copy.6 = bf16[1,384,2560]{1,2,0:T(8,128)(2,1)S(1)} copy(bf16[1,384,2560]{2,1,0:T(8,128)(2,1)} %all-gather.5.cloned.1.call-done) | data formatting | bytes 3932160 | tf_op jit(solution)/shard_map/all_gather | solution.py:31
  57.1 0.0 copy-done
  57.1 0.5 fusion.23
  57.6 0.3 fusion.4
  57.9 38.4 %all-gather.7.cloned.1.call-done = bf16[1,384,2560]{2,1,0:T(8,128)(2,1)} async-done(((bf16[1,24,2560]{2,1,0:T(8,128)(2,1)}), bf16[1,384,2560]{2,1,0:T(8,128)(2,1)}) %all-gather.7.cloned.1.call-update) | async-done | bytes 1966096 | tf_op jit(solution)/shard_map/all_gather | solution.py:32
  96.3 2.8 %copy.9 = bf16[1,384,2560]{1,2,0:T(8,128)(2,1)S(1)} copy(bf16[1,384,2560]{2,1,0:T(8,128)(2,1)} %all-gather.7.cloned.1.call-done) | data formatting | bytes 3932160 | tf_op jit(solution)/shard_map/all_gather | solution.py:32
  99.2 0.8 fusion.3
  100.0 0.7 copy.23
  (1 shorter events, 0.0 us)
Async XLA Ops:
  6.5 50.6 %copy-start = (bf16[24,2560]{1,0:T(8,128)(2,1)S(1)}, bf16[24,2560]{1,0:T(8,128)(2,1)}, u32[]{:S(2)}) copy-start(bf16[24,2560]{1,0:T(8,128)(2,1)} %param.4) | copy-start | bytes 368644
  6.5 47.7 %all-gather.5.cloned.1.call-start = ((), (), s32[]{:S(2)}) async-start(), calls=%async_computation | async-start | bytes 2088960 | tf_op jit(solution)/shard_map/all_gather | solution.py:31
  7.3 1.4 %copy-start.1 = (s32[2,24,2560]{2,1,0:T(8,128)S(1)}, s32[2,24,2560]{2,1,0:T(8,128)}, u32[]{:S(2)}) copy-start(s32[2,24,2560]{2,1,0:T(8,128)} %param.6) | copy-start | bytes 1474564
  7.3 1.4 %copy-start.2 = (bf16[2,24,2560]{2,1,0:T(8,128)(2,1)S(1)}, bf16[2,24,2560]{2,1,0:T(8,128)(2,1)}, u32[]{:S(2)}) copy-start(bf16[2,24,2560]{2,1,0:T(8,128)(2,1)} %param.5) | copy-start | bytes 737284
  10.6 85.8 %all-gather.7.cloned.1.call-start = ((), (), s32[]{:S(2)}) async-start(), calls=%async_computation.1 | async-start | bytes 2088960 | tf_op jit(solution)/shard_map/all_gather | solution.py:32
Sparse Core Ops, SparseCore 0:
  10.7 43.5 all-gather.4
  56.5 39.7 all-gather.6
where the time goes:
time: 108 us
  waiting for transfers between devices  82 us (76%)
  between operations  13.5 us (12%)
  local copies, waits for them, and re-layouts  8.42 us (8%)
  other arithmetic  2.19 us (2%)
  matrix products  1.37 us (1%)
    all_gather x1, waiting for transfers between devices, per_device(): lax.all_gather(rebuilt[0], 'patch', axis=0, tiled=True)  42.9 us
    all_gather x1, waiting for transfers between devices, per_device(): lax.all_gather(rebuilt[1], 'patch', axis=0, tiled=True)  38.4 us
    all_gather x1, local copies, waits for them, and re-layouts, per_device(): lax.all_gather(rebuilt[0], 'patch', axis=0, tiled=True)  2.83 us
    all_gather x1, local copies, waits for them, and re-layouts, per_device(): lax.all_gather(rebuilt[1], 'patch', axis=0, tiled=True)  2.83 us
  transfers between devices with their start and end apart: 2, of which 2 were waited for; matrix products, arithmetic and copies ran while one was open for 3% of the time, Pallas kernels for 0%

commit v1 on v0

v1 whole, which is shorter than its diff:
```python
import functools
import math

import jax
import jax.numpy as jnp
from jax import lax
from jax.experimental import pallas as pl
from jax.experimental.pallas import tpu as pltpu
from jax.sharding import PartitionSpec as P

HEADS = 20
HD = 128
BLOCK = 32
MESH = pl.DeviceIdType.MESH


def spans(n):
    return max((HEADS * d + HEADS - 1) // n - HEADS * d // n + 1 for d in range(n))


def kernel(
    n, group, span,
    q_ref, stale_ref, codes_ref, scale_ref, out_ref,
    stale_v, codes_v, scale_v, own, kv_in, q_in, o_buf,
    in_sem, kv_send, kv_recv, q_send, q_recv, o_send, o_recv,
):
    per = HEADS // group
    blocks = n // group
    rows = q_ref.shape[0]
    req = lax.axis_index("req")
    me = lax.axis_index("patch")
    my_blk, my_pos = lax.div(me, group), lax.rem(me, group)

    def first_head(d):
        return jnp.minimum(lax.div(HEADS * d, n), HEADS - span)

    barrier = pltpu.get_barrier_semaphore()

    def greet(k, c):
        pl.semaphore_signal(
            barrier, inc=1, device_id=(req, lax.rem(me + k, n)), device_id_type=MESH
        )
        return c

    loads = [
        pltpu.make_async_copy(scale_ref, scale_v, in_sem.at[0]),
        pltpu.make_async_copy(codes_ref, codes_v, in_sem.at[1]),
        pltpu.make_async_copy(stale_ref, stale_v, in_sem.at[2]),
    ]
    for load in loads:
        load.start()
    lax.fori_loop(1, n, greet, 0)
    for load in loads:
        load.wait()

    spread = (
        lax.shift_right_logical(
            lax.broadcasted_iota(jnp.int32, (HEADS * HD // BLOCK, HEADS * HD), 1), 5
        )
        == lax.broadcasted_iota(jnp.int32, (HEADS * HD // BLOCK, HEADS * HD), 0)
    ).astype(jnp.float32).astype(jnp.bfloat16)
    for x in range(2):
        power = lax.shift_left(jnp.ones_like(scale_v[x]), scale_v[x])
        power = power.astype(jnp.float32).astype(jnp.bfloat16)
        block_scale = jnp.dot(power, spread, preferred_element_type=jnp.float32)
        for h in range(HEADS):
            lanes = slice(h * HD, (h + 1) * HD)
            code = codes_v[x, :, lanes]
            exponent = lax.shift_right_logical(code, 3) & 15
            mantissa = code & 7
            whole = jnp.where(exponent > 0, mantissa + 8, mantissa)
            whole = lax.shift_left(whole, jnp.maximum(exponent - 1, 0))
            whole = jnp.where(code >= 128, -whole, whole)
            residual = whole.astype(jnp.float32) * (block_scale[:, lanes] * 2.0**-25)
            kept = stale_v[x, :, lanes].astype(jnp.float32)
            own[h, x] = (kept + residual).astype(jnp.bfloat16)

    pl.semaphore_wait(barrier, n - 1)

    def kv_copy(d):
        return pltpu.make_async_remote_copy(
            src_ref=own.at[pl.ds(first_head(d), span)],
            dst_ref=kv_in.at[:, :, me],
            send_sem=kv_send.at[d],
            recv_sem=kv_recv.at[me],
            device_id=(req, d),
            device_id_type=MESH,
        )

    def send_kv(k, c):
        kv_copy(lax.rem(me + k, n)).start()
        return c

    own_kv = pltpu.make_async_copy(
        own.at[pl.ds(first_head(me), span)], kv_in.at[:, :, me], kv_recv.at[me]
    )

    def q_route(h):
        unit = h * blocks + my_blk
        d = lax.div(unit, per)
        return d, lax.rem(unit, per) * group + my_pos

    def q_lanes(ref, h):
        return ref.at[:, pl.ds(pl.multiple_of(h * HD, HD), HD)]

    def q_copy(h):
        d, slot = q_route(h)
        return pltpu.make_async_remote_copy(
            src_ref=q_lanes(q_ref, h), dst_ref=q_in.at[slot],
            send_sem=q_send.at[h], recv_sem=q_recv.at[slot],
            device_id=(req, d), device_id_type=MESH,
        )

    def q_local(h):
        d, slot = q_route(h)
        return pltpu.make_async_copy(q_lanes(q_ref, h), q_in.at[slot], q_recv.at[slot])

    def send_q(h, c):
        d, slot = q_route(h)

        @pl.when(d != me)
        def _():
            q_copy(h).start()

        @pl.when(d == me)
        def _():
            q_local(h).start()

        return c

    lax.fori_loop(0, HEADS, send_q, 0)
    lax.fori_loop(1, n, send_kv, 0)
    own_kv.start()

    def wait_q(slot, c):
        pltpu.make_async_copy(q_lanes(q_ref, 0), q_in.at[slot], q_recv.at[slot]).wait()
        return c

    def wait_kv(s, c):
        pltpu.make_async_copy(
            own.at[pl.ds(0, span)], kv_in.at[:, :, s], kv_recv.at[s]
        ).wait()
        return c

    lax.fori_loop(0, HEADS, wait_q, 0)
    lax.fori_loop(0, n, wait_kv, 0)

    def o_route(slot):
        t, i = divmod(slot, group)
        unit = me * per + t
        h = lax.div(unit, blocks)
        return h, lax.rem(unit, blocks) * group + i

    for t in range(per):
        h = lax.div(me * per + t, blocks)
        at = h - first_head(me)
        head_query = q_in[t * group:(t + 1) * group].astype(jnp.float32)
        head_query = head_query.reshape(group * rows, HD).astype(jnp.bfloat16)
        head_key = kv_in[at, 0].astype(jnp.float32).reshape(n * rows, HD).astype(jnp.bfloat16)
        head_value = kv_in[at, 1].astype(jnp.float32).reshape(n * rows, HD).astype(jnp.bfloat16)
        scores = lax.dot_general(
            head_query, head_key, (((1,), (1,)), ((), ())),
            preferred_element_type=jnp.float32,
        ) * (HD ** -0.5)
        weights = jnp.exp(scores - jnp.max(scores, axis=1, keepdims=True))
        total = jnp.sum(weights, axis=1, keepdims=True)
        summed = jnp.dot(
            weights.astype(jnp.bfloat16), head_value, preferred_element_type=jnp.float32
        )
        o_buf[t * group:(t + 1) * group] = (
            (summed / total).reshape(group, rows, HD).astype(jnp.bfloat16)
        )
        for i in range(group):
            slot = t * group + i
            h, d = o_route(slot)

            @pl.when(d != me)
            def _():
                pltpu.make_async_remote_copy(
                    src_ref=o_buf.at[slot], dst_ref=q_lanes(out_ref, h),
                    send_sem=o_send.at[slot], recv_sem=o_recv.at[h],
                    device_id=(req, d), device_id_type=MESH,
                ).start()

            @pl.when(d == me)
            def _():
                pltpu.make_async_copy(
                    o_buf.at[slot], q_lanes(out_ref, h), o_recv.at[h]
                ).start()

    def drain_kv(k, c):
        kv_copy(lax.rem(me + k, n)).wait_send()
        return c

    def drain_q(h, c):
        d, slot = q_route(h)

        @pl.when(d != me)
        def _():
            q_copy(h).wait_send()

        return c

    lax.fori_loop(1, n, drain_kv, 0)
    lax.fori_loop(0, HEADS, drain_q, 0)
    for slot in range(HEADS):
        h, d = o_route(slot)

        @pl.when(d != me)
        def _():
            pltpu.make_async_remote_copy(
                src_ref=o_buf.at[slot], dst_ref=q_lanes(out_ref, h),
                send_sem=o_send.at[slot], recv_sem=o_recv.at[h],
                device_id=(req, d), device_id_type=MESH,
            ).wait_send()

    def wait_o(h, c):
        pltpu.make_async_copy(o_buf.at[0], q_lanes(out_ref, h), o_recv.at[h]).wait()
        return c

    lax.fori_loop(0, HEADS, wait_o, 0)


def solution(mesh):
    n = mesh.shape["patch"]
    group = math.gcd(HEADS, n)
    span = spans(n)

    def per_device(queries, stale_kv, residual_codes, scale_exponents):
        rows = queries.shape[0]
        anywhere = pl.BlockSpec(memory_space=pl.ANY)
        bf16, dma = jnp.bfloat16, pltpu.SemaphoreType.DMA
        return pl.pallas_call(
            functools.partial(kernel, n, group, span),
            out_shape=jax.ShapeDtypeStruct(queries.shape, bf16),
            in_specs=[anywhere] * 4,
            out_specs=anywhere,
            scratch_shapes=[
                pltpu.VMEM(stale_kv.shape, bf16),
                pltpu.VMEM(residual_codes.shape, jnp.int32),
                pltpu.VMEM(scale_exponents.shape, jnp.int32),
                pltpu.VMEM((HEADS, 2, rows, HD), bf16),
                pltpu.VMEM((span, 2, n, rows, HD), bf16),
                pltpu.VMEM((HEADS, rows, HD), bf16),
                pltpu.VMEM((HEADS, rows, HD), bf16),
                dma((3,)),
                dma((n,)), dma((n,)),
                dma((HEADS,)), dma((HEADS,)),
                dma((HEADS,)), dma((HEADS,)),
            ],
            compiler_params=pltpu.CompilerParams(
                collective_id=0, has_side_effects=True, vmem_limit_bytes=48 << 20
            ),
        )(queries, stale_kv, residual_codes, scale_exponents)

    return jax.shard_map(
        per_device,
        mesh=mesh,
        in_specs=(
            P(("req", "patch"), None),
            P(None, ("req", "patch"), None),
            P(None, ("req", "patch"), None),
            P(None, ("req", "patch"), None),
        ),
        out_specs=P(("req", "patch"), None),
        check_vma=False,
    )
```

time: 108 us -> 30.9 us (0.29)
  waiting for transfers between devices: 82 us -> 0 us
  Pallas kernels: 0 us -> 26.4 us
  between operations: 13.5 us -> 0.01 us
  local copies, waits for them, and re-layouts: 8.42 us -> 4.26 us
  other arithmetic: 2.19 us -> 0 us
  matrix products: 1.37 us -> 0 us
    all_gather x2 -> x0, waiting for transfers between devices: 81.3 us -> none  [the longest x1 42.9 us: per_device(): lax.all_gather(rebuilt[0], 'patch', axis=0, tiled=True)]
    pallas_call x0 -> x1, Pallas kernels: none -> 26.4 us  [per_device(): pl.pallas_call(functools.partial(kernel, n, group, span), out_shape=jax.S...]
    all_gather x2 -> x0, local copies, waits for them, and re-layouts: 5.65 us -> none  [the longest x1 2.83 us: per_device(): lax.all_gather(rebuilt[0], 'patch', axis=0, tiled=True)]
    unnamed x6 -> x9, local copies, waits for them, and re-layouts: 0.02 us -> 4.26 us
    dot_general x2 -> x0, matrix products: 1.37 us -> none  [the longest x1 0.84 us: per_device(): jnp.einsum('hqk,khd->hqd', weights_exp.astype(jnp.bfloat16), value_piece,...]
    mul x2 -> x0, local copies, waits for them, and re-layouts: 1.35 us -> none  [decode_residual(): return (shaped * block_scale[..., None]).reshape(residual_codes.shape)]
    convert_element_type x1 -> x0, other arithmetic: 1.1 us -> none  [per_device(): rebuilt = (stale_kv.astype(jnp.float32) + residual).astype(jnp.bfloat16)]
  transfers between devices with their start and end apart: 2 -> 0, of which waited for: 2 -> 0; matrix products, arithmetic and copies ran while one was open for 3% -> 0% of each run, Pallas kernels for 0% -> 0%
where the time goes in v1:
time: 30.9 us; the launch traced here: 30.7 us
  Pallas kernels  26.4 us (85%)
  local copies, waits for them, and re-layouts  4.26 us (14%)
    pallas_call x1, Pallas kernels, per_device(): pl.pallas_call(functools.partial(kernel, n, group, span), out_shape=jax.S...  26.4 us
    unnamed x9, local copies, waits for them, and re-layouts  4.26 us

profile of v1, /device:TPU:0, one launch (start us, length us, event | category | flops | bytes accessed | tf_op | source)
XLA Modules:
  0.0 30.7 jit_solution(14839640958072729836)
XLA Ops:
  0.0 0.0 copy-start
  0.0 1.0 %copy-done = s32[2,24,2560]{2,1,0:T(8,128)S(1)} copy-done((s32[2,24,2560]{2,1,0:T(8,128)S(1)}, s32[2,24,2560]{2,1,0:T(8,128)}, u32[]{:S(2)}) %copy-start) | copy-done | bytes 491544
  1.0 0.0 copy-start.1
  1.0 0.9 %copy-done.1 = bf16[2,24,2560]{2,1,0:T(8,128)(2,1)S(1)} copy-done((bf16[2,24,2560]{2,1,0:T(8,128)(2,1)S(1)}, bf16[2,24,2560]{2,1,0:T(8,128)(2,1)}, u32[]{:S(2)}) %copy-start.1) | copy-done | bytes 245784
  2.0 0.0 copy-start.2
  2.0 0.9 %copy-done.2 = bf16[24,2560]{1,0:T(8,128)(2,1)S(1)} copy-done((bf16[24,2560]{1,0:T(8,128)(2,1)S(1)}, bf16[24,2560]{1,0:T(8,128)(2,1)}, u32[]{:S(2)}) %copy-start.2) | copy-done | bytes 122904
  2.9 0.0 copy-start.3
  2.9 0.7 %copy-done.3 = s32[2,24,80]{2,1,0:T(8,128)S(1)} copy-done((s32[2,24,80]{2,1,0:T(8,128)S(1)}, s32[2,24,80]{2,1,0:T(8,128)}, u32[]{:S(2)}) %copy-start.3) | copy-done | bytes 15384
  3.6 26.4 %shard_map.46 = bf16[24,2560]{1,0:T(8,128)(2,1)S(1)} custom-call(bf16[24,2560]{1,0:T(8,128)(2,1)S(1)} %copy-done.2, bf16[2,24,2560]{2,1,0:T(8,128)(2,1)S(1)} %copy-done.1, s32[2,24,2560]{2,1,0:T(8,128)S(1)} %copy-done, s32[2,24,80]{2,1,0:T(8,128)S(1)} %copy-done.3), custom_call_target="tpu_custom_call" | custom-call | tf_op jit(solution)/shard_map/pallas_call | solution.py:233
  30.0 0.7 %copy.6 = bf16[24,2560]{1,0:T(8,128)(2,1)} copy(bf16[24,2560]{1,0:T(8,128)(2,1)S(1)} %shard_map.46) | data formatting | bytes 245760
Async XLA Ops:
  0.0 1.0 %copy-start = (s32[2,24,2560]{2,1,0:T(8,128)S(1)}, s32[2,24,2560]{2,1,0:T(8,128)}, u32[]{:S(2)}) copy-start(s32[2,24,2560]{2,1,0:T(8,128)} %codes_ref.1) | copy-start | bytes 1474564
  1.0 0.9 %copy-start.1 = (bf16[2,24,2560]{2,1,0:T(8,128)(2,1)S(1)}, bf16[2,24,2560]{2,1,0:T(8,128)(2,1)}, u32[]{:S(2)}) copy-start(bf16[2,24,2560]{2,1,0:T(8,128)(2,1)} %stale_ref.1) | copy-start | bytes 737284
  2.0 0.9 %copy-start.2 = (bf16[24,2560]{1,0:T(8,128)(2,1)S(1)}, bf16[24,2560]{1,0:T(8,128)(2,1)}, u32[]{:S(2)}) copy-start(bf16[24,2560]{1,0:T(8,128)(2,1)} %q_ref.1) | copy-start | bytes 368644
  2.9 0.7 %copy-start.3 = (s32[2,24,80]{2,1,0:T(8,128)S(1)}, s32[2,24,80]{2,1,0:T(8,128)}, u32[]{:S(2)}) copy-start(s32[2,24,80]{2,1,0:T(8,128)} %scale_ref.1) | copy-start | bytes 46084

commit v2 on v1

--- a/solution.py
+++ b/solution.py
@@ -228,13 +228,13 @@
 
     def per_device(queries, stale_kv, residual_codes, scale_exponents):
         rows = queries.shape[0]
-        anywhere = pl.BlockSpec(memory_space=pl.ANY)
+        far = pl.BlockSpec(memory_space=pltpu.HBM)
         bf16, dma = jnp.bfloat16, pltpu.SemaphoreType.DMA
         return pl.pallas_call(
             functools.partial(kernel, n, group, span),
             out_shape=jax.ShapeDtypeStruct(queries.shape, bf16),
-            in_specs=[anywhere] * 4,
-            out_specs=anywhere,
+            in_specs=[far] * 4,
+            out_specs=pl.BlockSpec(memory_space=pl.ANY),
             scratch_shapes=[
                 pltpu.VMEM(stale_kv.shape, bf16),
                 pltpu.VMEM(residual_codes.shape, jnp.int32),
@@ -249,7 +249,7 @@
                 dma((HEADS,)), dma((HEADS,)),
             ],
             compiler_params=pltpu.CompilerParams(
-                collective_id=0, has_side_effects=True, vmem_limit_bytes=48 << 20
+                collective_id=0, has_side_effects=True, vmem_limit_bytes=60 << 20
             ),
         )(queries, stale_kv, residual_codes, scale_exponents)
 

time: 30.9 us -> 27.7 us (0.90)
  local copies, waits for them, and re-layouts: 4.26 us -> 1.56 us
  Pallas kernels: 26.4 us -> 26 us
    unnamed x9 -> x1, local copies, waits for them, and re-layouts: 4.26 us -> 1.56 us
    pallas_call x1, Pallas kernels: 26.4 us -> 26 us  [per_device(): pl.pallas_call(functools.partial(kernel, n, group, span), out_shape=jax.S...]
where the time goes in v2:
time: 27.7 us; the launch traced here: 27.6 us
  Pallas kernels  26 us (94%)
  local copies, waits for them, and re-layouts  1.56 us (6%)
    pallas_call x1, Pallas kernels, per_device(): pl.pallas_call(functools.partial(kernel, n, group, span), out_shape=jax.S...  26 us
    unnamed x1, local copies, waits for them, and re-layouts  1.56 us

profile of v2, /device:TPU:0, one launch (start us, length us, event | category | flops | bytes accessed | tf_op | source)
XLA Modules:
  0.0 27.6 jit_solution(9373214066206680932)
XLA Ops:
  0.0 26.0 %shard_map.46 = bf16[24,2560]{1,0:T(8,128)(2,1)} custom-call(bf16[24,2560]{1,0:T(8,128)(2,1)} %q_ref.1, bf16[2,24,2560]{2,1,0:T(8,128)(2,1)} %stale_ref.1, s32[2,24,2560]{2,1,0:T(8,128)} %codes_ref.1, s32[2,24,80]{2,1,0:T(8,128)} %scale_ref.1), custom_call_target="tpu_custom_call" | custom-call | tf_op jit(solution)/shard_map/pallas_call | solution.py:233
  26.0 1.6 %copy.6 = bf16[24,2560]{1,0:T(8,128)(2,1)} copy(bf16[24,2560]{1,0:T(8,128)(2,1)} %shard_map.46) | data formatting | bytes 245760

commit v3 on v2

v3 whole, which is shorter than its diff:
```python
import functools
import math

import jax
import jax.numpy as jnp
from jax import lax
from jax.experimental import pallas as pl
from jax.experimental.pallas import tpu as pltpu
from jax.sharding import PartitionSpec as P

HEADS = 20
HD = 128
BLOCK = 32
MESH = pl.DeviceIdType.MESH
VMEM_LIMIT = 60 << 20


def spans(n):
    return max((HEADS * d + HEADS - 1) // n - HEADS * d // n + 1 for d in range(n))


def shared_head_kernel(
    n, group, span,
    q_ref, stale_ref, codes_ref, scale_ref, out_ref,
    stale_v, codes_v, scale_v, own, kv_in, q_in, o_buf,
    in_sem, kv_send, kv_recv, q_send, q_recv, o_send, o_recv,
):
    per = HEADS // group
    blocks = n // group
    rows = q_ref.shape[0]
    req = lax.axis_index("req")
    me = lax.axis_index("patch")
    my_blk, my_pos = lax.div(me, group), lax.rem(me, group)

    def first_head(d):
        return jnp.minimum(lax.div(HEADS * d, n), HEADS - span)

    barrier = pltpu.get_barrier_semaphore()

    def greet(k, c):
        pl.semaphore_signal(
            barrier, inc=1, device_id=(req, lax.rem(me + k, n)), device_id_type=MESH
        )
        return c

    loads = [
        pltpu.make_async_copy(scale_ref, scale_v, in_sem.at[0]),
        pltpu.make_async_copy(codes_ref, codes_v, in_sem.at[1]),
        pltpu.make_async_copy(stale_ref, stale_v, in_sem.at[2]),
    ]
    for load in loads:
        load.start()
    lax.fori_loop(1, n, greet, 0)
    for load in loads:
        load.wait()

    def store(h, x, value):
        own[h, x] = value

    decode(codes_v, stale_v, scale_v, store)
    pl.semaphore_wait(barrier, n - 1)

    def kv_copy(d):
        return pltpu.make_async_remote_copy(
            src_ref=own.at[pl.ds(first_head(d), span)],
            dst_ref=kv_in.at[:, :, me],
            send_sem=kv_send.at[d],
            recv_sem=kv_recv.at[me],
            device_id=(req, d),
            device_id_type=MESH,
        )

    def send_kv(k, c):
        kv_copy(lax.rem(me + k, n)).start()
        return c

    own_kv = pltpu.make_async_copy(
        own.at[pl.ds(first_head(me), span)], kv_in.at[:, :, me], kv_recv.at[me]
    )

    def q_route(h):
        unit = h * blocks + my_blk
        d = lax.div(unit, per)
        return d, lax.rem(unit, per) * group + my_pos

    def q_lanes(ref, h):
        return ref.at[:, pl.ds(pl.multiple_of(h * HD, HD), HD)]

    def q_copy(h):
        d, slot = q_route(h)
        return pltpu.make_async_remote_copy(
            src_ref=q_lanes(q_ref, h), dst_ref=q_in.at[slot],
            send_sem=q_send.at[h], recv_sem=q_recv.at[slot],
            device_id=(req, d), device_id_type=MESH,
        )

    def q_local(h):
        d, slot = q_route(h)
        return pltpu.make_async_copy(q_lanes(q_ref, h), q_in.at[slot], q_recv.at[slot])

    def send_q(h, c):
        d, slot = q_route(h)

        @pl.when(d != me)
        def _():
            q_copy(h).start()

        @pl.when(d == me)
        def _():
            q_local(h).start()

        return c

    lax.fori_loop(0, HEADS, send_q, 0)
    lax.fori_loop(1, n, send_kv, 0)
    own_kv.start()

    def wait_q(slot, c):
        pltpu.make_async_copy(q_lanes(q_ref, 0), q_in.at[slot], q_recv.at[slot]).wait()
        return c

    def wait_kv(s, c):
        pltpu.make_async_copy(
            own.at[pl.ds(0, span)], kv_in.at[:, :, s], kv_recv.at[s]
        ).wait()
        return c

    lax.fori_loop(0, HEADS, wait_q, 0)
    lax.fori_loop(0, n, wait_kv, 0)

    def o_route(slot):
        t, i = divmod(slot, group)
        unit = me * per + t
        h = lax.div(unit, blocks)
        return h, lax.rem(unit, blocks) * group + i

    for t in range(per):
        h = lax.div(me * per + t, blocks)
        at = h - first_head(me)
        head_query = q_in[t * group:(t + 1) * group].astype(jnp.float32)
        head_query = head_query.reshape(group * rows, HD).astype(jnp.bfloat16)
        head_key = kv_in[at, 0].astype(jnp.float32).reshape(n * rows, HD).astype(jnp.bfloat16)
        head_value = kv_in[at, 1].astype(jnp.float32).reshape(n * rows, HD).astype(jnp.bfloat16)
        scores = lax.dot_general(
            head_query, head_key, (((1,), (1,)), ((), ())),
            preferred_element_type=jnp.float32,
        ) * (HD ** -0.5)
        weights = jnp.exp(scores - jnp.max(scores, axis=1, keepdims=True))
        total = jnp.sum(weights, axis=1, keepdims=True)
        summed = jnp.dot(
            weights.astype(jnp.bfloat16), head_value, preferred_element_type=jnp.float32
        )
        o_buf[t * group:(t + 1) * group] = (
            (summed / total).reshape(group, rows, HD).astype(jnp.bfloat16)
        )
        for i in range(group):
            slot = t * group + i
            h, d = o_route(slot)

            @pl.when(d != me)
            def _():
                pltpu.make_async_remote_copy(
                    src_ref=o_buf.at[slot], dst_ref=q_lanes(out_ref, h),
                    send_sem=o_send.at[slot], recv_sem=o_recv.at[h],
                    device_id=(req, d), device_id_type=MESH,
                ).start()

            @pl.when(d == me)
            def _():
                pltpu.make_async_copy(
                    o_buf.at[slot], q_lanes(out_ref, h), o_recv.at[h]
                ).start()

    def drain_kv(k, c):
        kv_copy(lax.rem(me + k, n)).wait_send()
        return c

    def drain_q(h, c):
        d, slot = q_route(h)

        @pl.when(d != me)
        def _():
            q_copy(h).wait_send()

        return c

    lax.fori_loop(1, n, drain_kv, 0)
    lax.fori_loop(0, HEADS, drain_q, 0)
    for slot in range(HEADS):
        h, d = o_route(slot)

        @pl.when(d != me)
        def _():
            pltpu.make_async_remote_copy(
                src_ref=o_buf.at[slot], dst_ref=q_lanes(out_ref, h),
                send_sem=o_send.at[slot], recv_sem=o_recv.at[h],
                device_id=(req, d), device_id_type=MESH,
            ).wait_send()

    def wait_o(h, c):
        pltpu.make_async_copy(o_buf.at[0], q_lanes(out_ref, h), o_recv.at[h]).wait()
        return c

    lax.fori_loop(0, HEADS, wait_o, 0)


def decode(codes_v, stale_v, scale_v, store):
    groups, width = HEADS * HD // BLOCK, HEADS * HD
    spread = (
        lax.shift_right_logical(lax.broadcasted_iota(jnp.int32, (groups, width), 1), 5)
        == lax.broadcasted_iota(jnp.int32, (groups, width), 0)
    ).astype(jnp.float32).astype(jnp.bfloat16)
    for x in range(2):
        power = lax.shift_left(jnp.ones_like(scale_v[x]), scale_v[x])
        power = power.astype(jnp.float32).astype(jnp.bfloat16)
        block_scale = jnp.dot(power, spread, preferred_element_type=jnp.float32)
        for h in range(HEADS):
            lanes = slice(h * HD, (h + 1) * HD)
            code = codes_v[x, :, lanes]
            exponent = lax.shift_right_logical(code, 3) & 15
            mantissa = code & 7
            whole = jnp.where(exponent > 0, mantissa + 8, mantissa)
            whole = lax.shift_left(whole, jnp.maximum(exponent - 1, 0))
            whole = jnp.where(code >= 128, -whole, whole)
            residual = whole.astype(jnp.float32) * (block_scale[:, lanes] * 2.0**-25)
            kept = stale_v[x, :, lanes].astype(jnp.float32)
            store(h, x, (kept + residual).astype(jnp.bfloat16))


def whole_head_kernel(
    n, heavy,
    q_ref, stale_ref, codes_ref, scale_ref, out_ref,
    q_v, stale_v, codes_v, scale_v, own, arrived, o_buf,
    in_sem, qkv_send, qkv_recv, o_send, o_recv,
):
    rows = q_ref.shape[0]
    base = HEADS // n
    most = arrived.shape[0]
    req = lax.axis_index("req")
    me = lax.axis_index("patch")
    order = sorted(range(1, n), key=lambda k: abs(2 * k - n))

    def partner(k):
        d = me + k
        return jnp.where(d >= n, d - n, d)

    def first_head(d):
        return sum([jnp.where(d > e, 1, 0) for e in heavy], base * d)

    def is_heavy(d):
        return sum([jnp.where(d == e, 1, 0) for e in heavy], 0 * d) > 0

    def columns(ref, h, count):
        return ref.at[:, pl.ds(pl.multiple_of(h * HD, HD), count * HD)]

    loads = [
        pltpu.make_async_copy(a, b, in_sem.at[i])
        for i, (a, b) in enumerate(
            [(scale_ref, scale_v), (codes_ref, codes_v), (stale_ref, stale_v), (q_ref, q_v)]
        )
    ]
    for load in loads:
        load.start()
    barrier = pltpu.get_barrier_semaphore()
    for k in order:
        pl.semaphore_signal(
            barrier, inc=1, device_id=(req, partner(k)), device_id_type=MESH
        )
    for load in loads:
        load.wait()

    def store(h, x, value):
        own[h, 1 + x] = value

    decode(codes_v, stale_v, scale_v, store)
    for h in range(HEADS):
        own[h, 0] = q_v[:, h * HD:(h + 1) * HD]
    pl.semaphore_wait(barrier, n - 1)

    def for_head(slot, d, run):
        if slot < base:
            run()
        elif heavy:
            pl.when(is_heavy(d))(run)

    def send(slot, k):
        d = partner(k)
        return pltpu.make_async_remote_copy(
            src_ref=own.at[first_head(d) + slot],
            dst_ref=arrived.at[slot, :, me],
            send_sem=qkv_send.at[slot, k],
            recv_sem=qkv_recv.at[slot, me],
            device_id=(req, d),
            device_id_type=MESH,
        )

    def keep(slot):
        return pltpu.make_async_copy(
            own.at[first_head(me) + slot], arrived.at[slot, :, me], qkv_recv.at[slot, me]
        )

    def landed(slot, s):
        return pltpu.make_async_copy(own.at[0], arrived.at[slot, :, s], qkv_recv.at[slot, s])

    for k in order:
        for slot in range(most):
            for_head(slot, partner(k), lambda: send(slot, k).start())
    for slot in range(most):
        for_head(slot, me, lambda: keep(slot).start())

    def attend(slot):
        for s in range(n):
            landed(slot, s).wait()

        def flat(x):
            return arrived[slot, x].astype(jnp.float32).reshape(n * rows, HD).astype(jnp.bfloat16)

        scores = lax.dot_general(
            flat(0), flat(1), (((1,), (1,)), ((), ())), preferred_element_type=jnp.float32
        )
        top = jnp.max(scores, axis=1, keepdims=True)
        weights = jnp.exp((scores - top) * (HD ** -0.5))
        total = jnp.sum(weights, axis=1, keepdims=True)
        summed = jnp.dot(
            weights.astype(jnp.bfloat16), flat(2), preferred_element_type=jnp.float32
        )
        result = (summed / total).reshape(n, rows, HD).astype(jnp.bfloat16)
        o_buf[:, :, slot * HD:(slot + 1) * HD] = result

    for slot in range(most):
        for_head(slot, me, lambda: attend(slot))

    def give(k, count):
        return pltpu.make_async_remote_copy(
            src_ref=columns(o_buf.at[partner(k)], 0, count),
            dst_ref=columns(out_ref, first_head(me), count),
            send_sem=o_send.at[k],
            recv_sem=o_recv.at[me],
            device_id=(req, partner(k)),
            device_id_type=MESH,
        )

    def give_all(count):
        for k in order:
            give(k, count).start()
        pltpu.make_async_copy(
            columns(o_buf.at[me], 0, count),
            columns(out_ref, first_head(me), count),
            o_recv.at[me],
        ).start()

    def drain_all(count):
        for k in order:
            give(k, count).wait_send()

    def by_load(run):
        if heavy:
            pl.when(is_heavy(me))(lambda: run(base + 1))
            pl.when(jnp.logical_not(is_heavy(me)))(lambda: run(base))
        else:
            run(base)

    by_load(give_all)
    for k in order:
        for slot in range(most):
            for_head(slot, partner(k), lambda: send(slot, k).wait_send())
    for d in range(n):
        count = base + (d in heavy)
        pltpu.make_async_copy(
            columns(o_buf.at[0], 0, count), columns(out_ref, 0, count), o_recv.at[d]
        ).wait()
    by_load(drain_all)


def whole_heads(n, rows, specs, operands):
    extra = HEADS % n
    step = n // extra if extra else 1
    heavy = tuple(j * step + (j % 2) * (step // 2) for j in range(extra))
    most = HEADS // n + bool(extra)
    queries, stale_kv, residual_codes, scale_exponents = operands
    bf16, dma = jnp.bfloat16, pltpu.SemaphoreType.DMA
    return pl.pallas_call(
        functools.partial(whole_head_kernel, n, heavy),
        out_shape=jax.ShapeDtypeStruct(queries.shape, bf16),
        scratch_shapes=[
            pltpu.VMEM(queries.shape, bf16),
            pltpu.VMEM(stale_kv.shape, bf16),
            pltpu.VMEM(residual_codes.shape, jnp.int32),
            pltpu.VMEM(scale_exponents.shape, jnp.int32),
            pltpu.VMEM((HEADS, 3, rows, HD), bf16),
            pltpu.VMEM((most, 3, n, rows, HD), bf16),
            pltpu.VMEM((n, rows, most * HD), bf16),
            dma((4,)),
            dma((most, n)), dma((most, n)),
            dma((n,)), dma((n,)),
        ],
        compiler_params=pltpu.CompilerParams(
            collective_id=0, has_side_effects=True, vmem_limit_bytes=VMEM_LIMIT
        ),
        **specs,
    )(*operands)


def solution(mesh):
    n = mesh.shape["patch"]
    group = math.gcd(HEADS, n)
    span = spans(n)

    def per_device(queries, stale_kv, residual_codes, scale_exponents):
        rows = queries.shape[0]
        specs = dict(
            in_specs=[pl.BlockSpec(memory_space=pltpu.HBM)] * 4,
            out_specs=pl.BlockSpec(memory_space=pl.ANY),
        )
        operands = (queries, stale_kv, residual_codes, scale_exponents)
        if n <= HEADS:
            return whole_heads(n, rows, specs, operands)
        bf16, dma = jnp.bfloat16, pltpu.SemaphoreType.DMA
        return pl.pallas_call(
            functools.partial(shared_head_kernel, n, group, span),
            out_shape=jax.ShapeDtypeStruct(queries.shape, bf16),
            scratch_shapes=[
                pltpu.VMEM(stale_kv.shape, bf16),
                pltpu.VMEM(residual_codes.shape, jnp.int32),
                pltpu.VMEM(scale_exponents.shape, jnp.int32),
                pltpu.VMEM((HEADS, 2, rows, HD), bf16),
                pltpu.VMEM((span, 2, n, rows, HD), bf16),
                pltpu.VMEM((HEADS, rows, HD), bf16),
                pltpu.VMEM((HEADS, rows, HD), bf16),
                dma((3,)),
                dma((n,)), dma((n,)),
                dma((HEADS,)), dma((HEADS,)),
                dma((HEADS,)), dma((HEADS,)),
            ],
            compiler_params=pltpu.CompilerParams(
                collective_id=0, has_side_effects=True, vmem_limit_bytes=VMEM_LIMIT
            ),
            **specs,
        )(*operands)

    return jax.shard_map(
        per_device,
        mesh=mesh,
        in_specs=(
            P(("req", "patch"), None),
            P(None, ("req", "patch"), None),
            P(None, ("req", "patch"), None),
            P(None, ("req", "patch"), None),
        ),
        out_specs=P(("req", "patch"), None),
        check_vma=False,
    )
```

time: 27.7 us -> 24.6 us (0.89)
  Pallas kernels: 26 us -> 22.8 us
    pallas_call x1, Pallas kernels: 26 us -> 22.8 us  [whole_heads(): pl.pallas_call(functools.partial(whole_head_kernel, n, heavy), out_shape=...]
where the time goes in v3:
time: 24.6 us; the launch traced here: 24.4 us
  Pallas kernels  22.8 us (93%)
  local copies, waits for them, and re-layouts  1.56 us (6%)
    pallas_call x1, Pallas kernels, whole_heads(): pl.pallas_call(functools.partial(whole_head_kernel, n, heavy), out_shape=...  22.8 us
    unnamed x1, local copies, waits for them, and re-layouts  1.56 us

profile of v3, /device:TPU:0, one launch (start us, length us, event | category | flops | bytes accessed | tf_op | source)
XLA Modules:
  0.0 24.4 jit_solution(2933372812233812765)
XLA Ops:
  0.0 22.8 %shard_map.46 = bf16[24,2560]{1,0:T(8,128)(2,1)} custom-call(bf16[24,2560]{1,0:T(8,128)(2,1)} %q_ref.1, bf16[2,24,2560]{2,1,0:T(8,128)(2,1)} %stale_ref.1, s32[2,24,2560]{2,1,0:T(8,128)} %codes_ref.1, s32[2,24,80]{2,1,0:T(8,128)} %scale_ref.1), custom_call_target="tpu_custom_call" | custom-call | tf_op jit(solution)/shard_map/pallas_call | solution.py:382
  22.9 1.6 %copy.6 = bf16[24,2560]{1,0:T(8,128)(2,1)} copy(bf16[24,2560]{1,0:T(8,128)(2,1)} %shard_map.46) | data formatting | bytes 245760

commit v4 on v3

--- a/solution.py
+++ b/solution.py
@@ -238,7 +238,7 @@
     most = arrived.shape[0]
     req = lax.axis_index("req")
     me = lax.axis_index("patch")
-    order = sorted(range(1, n), key=lambda k: abs(2 * k - n))
+    order = sorted(range(1, n), key=lambda k: -abs(2 * k - n))
 
     def partner(k):
         d = me + k

time: 24.6 us -> 23.1 us (0.939)
  Pallas kernels: 22.8 us -> 21.4 us
    pallas_call x1, Pallas kernels: 22.8 us -> 21.4 us  [whole_heads(): pl.pallas_call(functools.partial(whole_head_kernel, n, heavy), out_shape=...]
where the time goes in v4:
time: 23.1 us; the launch traced here: 22.9 us
  Pallas kernels  21.4 us (93%)
  local copies, waits for them, and re-layouts  1.56 us (7%)
    pallas_call x1, Pallas kernels, whole_heads(): pl.pallas_call(functools.partial(whole_head_kernel, n, heavy), out_shape=...  21.4 us
    unnamed x1, local copies, waits for them, and re-layouts  1.56 us

profile of v4, /device:TPU:0, one launch (start us, length us, event | category | flops | bytes accessed | tf_op | source)
XLA Modules:
  0.0 22.9 jit_solution(9606251523025127443)
XLA Ops:
  0.0 21.4 %shard_map.46 = bf16[24,2560]{1,0:T(8,128)(2,1)} custom-call(bf16[24,2560]{1,0:T(8,128)(2,1)} %q_ref.1, bf16[2,24,2560]{2,1,0:T(8,128)(2,1)} %stale_ref.1, s32[2,24,2560]{2,1,0:T(8,128)} %codes_ref.1, s32[2,24,80]{2,1,0:T(8,128)} %scale_ref.1), custom_call_target="tpu_custom_call" | custom-call | tf_op jit(solution)/shard_map/pallas_call | solution.py:382
  21.4 1.6 %copy.6 = bf16[24,2560]{1,0:T(8,128)(2,1)} copy(bf16[24,2560]{1,0:T(8,128)(2,1)} %shard_map.46) | data formatting | bytes 245760
